TPU v7x, 32 devices: a whole 2x2x4 slice. The times are simulated.
32 devices in a mesh: parts: 2 (over x), rows: 8 (over z, y), aux: 2 (over core).
Axes of the slice: x: 2, y: 2, z: 4, core: 2. Of those that a mesh axis runs over, the one named last changes fastest.
Arguments:
- integrals: bfloat16 [4, 2048, 2048], P(('parts', 'aux'), 'rows'), parts along dimension 0, may hold values from -6 to 6
- coefficients: bfloat16 [4096, 256], P(('parts', 'rows')), parts along dimension 0, may hold values from -0.046875 to 0.046875
- screen: int32 [4, 8, 8], P(('parts', 'aux'), 'rows'), parts along dimension 0, may hold values 0 or 1
Outputs:
- exchange: bfloat16 [4096, 2048], P(('parts', 'rows'), 'aux'), parts along dimension 0
There are 2 independent parts, one for each index of `parts`. A program takes and returns all parts, laid end to end along the dimension named above; each array names one. Nothing has to cross between parts.
All inputs are finite; a program needn't handle non-finite values. No bound on the sum of `screen` on one device may be relied on, other than what follows from the above.
Results may differ from a plain program's by a relative error of at most 0.0061.
Values may be sent and summed in bfloat16 or wider, within the bound.
A program may use at most 128 MiB of HBM per device.

v0:
```python
import jax
import jax.numpy as jnp
from jax import lax
from jax.sharding import PartitionSpec as P


def local(integrals, coefficients, screen):
    block = coefficients.shape[0]
    blocks_all = screen.shape[2]
    tiles = screen[0, 0].astype(jnp.float32)
    piece = lax.all_gather(coefficients, "rows", axis=0, tiled=True)
    count = piece.shape[0]
    owner = jnp.arange(count, dtype=jnp.int32) // block
    onehot = (owner[:, None] == jnp.arange(blocks_all, dtype=jnp.int32)[None, :]).astype(
        jnp.float32
    )
    weights = jnp.dot(onehot, tiles, precision=lax.Precision.HIGHEST).astype(jnp.bfloat16)
    masked = integrals * weights[None, None, :]
    half_sum = jnp.einsum("abl,lo->abo", masked, piece, preferred_element_type=jnp.float32)
    half = half_sum.astype(jnp.bfloat16)
    partial_rows = jnp.einsum(
        "amo,ano->mn",
        half,
        lax.all_gather(half, "rows", axis=1, tiled=True),
        preferred_element_type=jnp.float32,
    )
    return lax.psum_scatter(
        partial_rows.astype(jnp.bfloat16), "aux", scatter_dimension=1, tiled=True
    )


def solution(mesh):
    in_specs = (
        P(("parts", "aux"), "rows", None),
        P(("parts", "rows"), None),
        P(("parts", "aux"), "rows", None),
    )
    out_specs = P(("parts", "rows"), "aux")
    return jax.shard_map(local, mesh=mesh, in_specs=in_specs, out_specs=out_specs, check_vma=False)
```

profile of v0, /device:TPU:1, one launch (start us, length us, event | category | flops | bytes accessed | tf_op | source)
XLA Modules:
  0.0 110.6 jit_solution(10436313049674296749)
XLA Ops:
  6.5 0.0 all-gather.4.cloned.1.call-start
  6.5 0.7 all-gather.4.cloned.1.call-update
  7.3 0.0 all-gather.6.cloned.1.call-start
  7.3 1.4 %fusion.2 = f32[1,2048]{1,0:T(1,128)S(1)} fusion(s32[2048]{0:T(1024)S(1)} %add_select_fusion, s32[1,1,8]{2,1,0:T(1,128)} %param.5), kind=kOutput, calls=%fused_computation.5 | convolution fusion | flops 213000 | bytes 16416 | tf_op jit(solution)/shard_map/dot_general | solution.py:17
  8.7 42.1 %all-gather.4.cloned.1.call-done = bf16[2048,256]{1,0:T(8,128)(2,1)} async-done(((bf16[256,256]{1,0:T(8,128)(2,1)}), bf16[2048,256]{1,0:T(8,128)(2,1)}) %all-gather.4.cloned.1.call-update) | async-done | bytes 1048592 | tf_op jit(solution)/shard_map/all_gather | solution.py:11
  50.7 2.6 %convolution_convert_fusion.1 = bf16[256,256]{1,0:T(8,128)(2,1)} fusion(bf16[2048,256]{1,0:T(8,128)(2,1)} %all-gather.4.cloned.1.call-done, bf16[1,256,2048]{2,1,0:T(8,128)(2,1)} %param.3, bf16[2048]{0:T(1024)(128)(2,1)S(1)} %convert_element_type.21), kind=kOutput, calls=%fused_computation.1 | convolution fusion | flops 269025280 | bytes 2232320 | tf_op jit(solution)/shard_map/abl,lo->abo/dot_general | solution.py:19
  53.4 0.0 all-gather.6.cloned.1.call-update
  53.4 0.0 reduce-scatter.2.cloned.1.call-start
  53.5 39.0 %all-gather.6.cloned.1.call-done = bf16[2048,256]{1,0:T(8,128)(2,1)} async-done(((bf16[256,256]{1,0:T(8,128)(2,1)}), bf16[2048,256]{1,0:T(8,128)(2,1)}) %all-gather.6.cloned.1.call-update) | async-done | bytes 1048592 | tf_op jit(solution)/shard_map/all_gather | solution.py:24
  92.5 2.8 %convolution_convert_fusion = bf16[256,2048]{1,0:T(8,128)(2,1)} fusion(bf16[256,256]{1,0:T(8,128)(2,1)} %convolution_convert_fusion.1, bf16[2048,256]{1,0:T(8,128)(2,1)} %all-gather.6.cloned.1.call-done), kind=kOutput, calls=%fused_computation | convolution fusion | flops 268959744 | bytes 2228224 | tf_op jit(solution)/shard_map/amo,ano->mn/dot_general | solution.py:21
  95.3 0.0 reduce-scatter.2.cloned.1.call-update
  95.3 8.8 %reduce-scatter.2.cloned.1.call-done = bf16[256,1024]{1,0:T(8,128)(2,1)} async-done(((bf16[256,2048]{1,0:T(8,128)(2,1)}), bf16[256,1024]{1,0:T(8,128)(2,1)}) %reduce-scatter.2.cloned.1.call-update) | async-done | bytes 524304 | tf_op jit(solution)/shard_map/reduce_scatter | solution.py:27
  (2 shorter events, 0.0 us)
Async XLA Ops:
  6.5 44.2 %all-gather.4.cloned.1.call-start = ((), (), s32[]{:S(2)}) async-start(), calls=%async_computation.1 | async-start | bytes 1179648 | tf_op jit(solution)/shard_map/all_gather | solution.py:11
  7.3 85.2 %all-gather.6.cloned.1.call-start = ((), (), s32[]{:S(2)}) async-start(), calls=%async_computation.3 | async-start | bytes 1179648 | tf_op jit(solution)/shard_map/all_gather | solution.py:24
  53.4 50.7 %reduce-scatter.2.cloned.1.call-start = ((), (), s32[]{:S(2)}) async-start(), calls=%async_computation.2 | async-start | bytes 1572864 | tf_op jit(solution)/shard_map/reduce_scatter | solution.py:27
Sparse Core Ops, SparseCore 0:
  9.5 41.2 all-gather.3
  53.5 38.8 all-gather.5
  95.4 8.6 reduce-scatter.1
where the time goes:
time: 111 us
  waiting for transfers between devices  90.6 us (82%)
  between operations  13.1 us (12%)
  matrix products  6.82 us (6%)
    all_gather x1, waiting for transfers between devices, local(): piece = lax.all_gather(coefficients, 'rows', axis=0, tiled=True)  42.1 us
    all_gather x1, waiting for transfers between devices, local(): lax.all_gather(half, 'rows', axis=1, tiled=True)  39 us
    reduce_scatter x1, waiting for transfers between devices, local(): lax.psum_scatter(partial_rows.astype(jnp.bfloat16), 'aux', scatter_dimens...  8.8 us
    dot_general x1, matrix products, local(): jnp.einsum('amo,ano->mn', half, lax.all_gather(half, 'rows', axis=1, tile...  2.81 us
    dot_general x1, matrix products, local(): jnp.einsum('abl,lo->abo', masked, piece, preferred_element_type=jnp.float32)  2.64 us
  transfers between devices with their start and end apart: 3, of which 3 were waited for; matrix products, arithmetic and copies ran while one was open for 1% of the time, Pallas kernels for 0%

commit v1 on v0

v1 whole, which is shorter than its diff:
```python
import functools

import jax
import jax.numpy as jnp
from jax import lax
from jax.experimental import pallas as pl
from jax.experimental.pallas import tpu as pltpu
from jax.sharding import PartitionSpec as P

MESH = pl.DeviceIdType.MESH


def split_rows(n):
    inner = 1
    while inner * inner * 4 <= n:
        inner *= 2
    return n // inner, inner


def table(outer, rank, z):
    code = 0
    for place in range(outer):
        others = sorted((k for k in range(outer) if k != place), key=lambda k: (abs(k - place), k))
        code += others[rank] * outer**place
    power = 1
    bit = 1
    while bit < outer:
        power = power * (1 + (outer**bit - 1) * ((z // bit) % 2))
        bit *= 2
    return (code // power) % outer


def remote(src, dst, send, recv, rows, aux):
    return pltpu.make_async_remote_copy(
        src_ref=src,
        dst_ref=dst,
        send_sem=send,
        recv_sem=recv,
        device_id={"rows": rows, "aux": aux},
        device_id_type=MESH,
    )


def kernel(
    outer,
    inner,
    a_hbm,
    c_hbm,
    screen,
    out_hbm,
    a,
    c,
    acc,
    left,
    h,
    out,
    load_sem,
    store_sem,
    cz_send,
    cz_recv,
    cy_send,
    cy_recv,
    cs_send,
    cs_recv,
    hs_send,
    hs_recv,
    hz_send,
    hz_recv,
    hy_send,
    hf_send,
    hy_recv,
):
    n = outer * inner
    block = c_hbm.shape[0]
    part = block // 2
    ho = outer // 2
    me = lax.axis_index("rows")
    core = lax.axis_index("aux")
    sib = 1 - core
    z = me // inner
    y = me % inner
    owner = z // ho

    load_a = pltpu.make_async_copy(a_hbm.at[0], a, load_sem.at[0])
    load_c = pltpu.make_async_copy(c_hbm, c.at[me], load_sem.at[1])
    load_c.start()
    load_a.start()

    zs = [table(outer, rank, z) for rank in range(outer - 1)]
    ys = [(y + k) % inner for k in range(1, inner)]

    barrier = pltpu.get_barrier_semaphore()
    for k in range(2):
        for other in zs:
            pl.semaphore_signal(
                barrier, inc=1, device_id={"rows": other * inner + y, "aux": k}, device_id_type=MESH
            )
        for other in ys:
            pl.semaphore_signal(
                barrier, inc=1, device_id={"rows": z * inner + other, "aux": k}, device_id_type=MESH
            )
    pl.semaphore_signal(barrier, inc=1, device_id={"rows": me, "aux": sib}, device_id_type=MESH)
    pl.semaphore_wait(barrier, 2 * (outer - 1) + 2 * (inner - 1) + 1)

    def piece(s, half):
        return c.at[s, pl.ds(pl.multiple_of(half * part, part), part)]

    sends = []

    def c_along_z(other):
        own = piece(me, core)
        copy = remote(own, own, cz_send.at[other], cz_recv.at[z], other * inner + y, core)
        copy.start()
        sends.append(copy)

    def c_along_y(source):
        block_at = piece(source * inner + y, core)
        for other in ys:
            copy = remote(
                block_at,
                block_at,
                cy_send.at[source, other],
                cy_recv.at[source, y],
                z * inner + other,
                core,
            )
            copy.start()
            sends.append(copy)

    def c_to_sibling(s):
        block_at = piece(s, core)
        copy = remote(block_at, block_at, cs_send.at[s], cs_recv.at[s], me, sib)
        copy.start()
        sends.append(copy)

    def wait_recv(ref, sem):
        remote(ref, ref, cz_send.at[0], sem, me, sib).wait_recv()

    load_c.wait()
    c_along_y(z)
    for other in zs:
        c_along_z(other)
    load_a.wait()

    def product(s):
        columns = pl.ds(pl.multiple_of(s * block, block), block)
        flag = screen[0, 0, s].astype(jnp.float32)
        return flag * jnp.dot(a[:, columns], c[s], preferred_element_type=jnp.float32)

    acc[...] = product(me)

    for source in zs:
        wait_recv(piece(source * inner + y, core), cz_recv.at[source])
        c_along_y(source)
        c_to_sibling(source * inner + y)
    for source in zs:
        s = source * inner + y
        wait_recv(piece(s, sib), cs_recv.at[s])
        acc[...] += product(s)
    arrivals = [(source, other) for source in [z] + zs for other in ys]
    for source, other in arrivals:
        s = source * inner + other
        wait_recv(piece(s, core), cy_recv.at[source, other])
        c_to_sibling(s)
    for source, other in arrivals:
        s = source * inner + other
        wait_recv(piece(s, sib), cs_recv.at[s])
        acc[...] += product(s)

    left[core] = acc[...].astype(left.dtype)

    mine = left.at[core]

    def slot(aux, source, yy):
        return h.at[aux, (source % ho) * inner + yy]

    for other in ys:
        copy = remote(
            mine, slot(core, z, y), hy_send.at[other], hy_recv.at[core, z, y], z * inner + other, owner
        )
        copy.start()
        sends.append(copy)
    for other in zs:
        copy = remote(
            mine, slot(core, z, y), hz_send.at[other], hz_recv.at[core, z], other * inner + y, owner
        )
        copy.start()
        sends.append(copy)
    to_sib = remote(mine, mine, hs_send.at[0], hs_recv.at[0], me, sib)
    to_sib.start()
    sends.append(to_sib)

    def forward(aux, source, other):
        ref = slot(aux, source, y)
        return remote(
            ref, ref, hf_send.at[aux, source, other], hy_recv.at[aux, source, y], z * inner + other, core
        )

    def emit(source, yy, right0, right1):
        at = (source % ho) * inner + yy
        nt = (((1,), (1,)), ((), ()))
        p0 = lax.dot_general(left[0], right0, nt, preferred_element_type=jnp.float32)
        p1 = lax.dot_general(left[1], right1, nt, preferred_element_type=jnp.float32)
        total = p0.astype(out.dtype).astype(jnp.float32) + p1.astype(out.dtype).astype(jnp.float32)
        columns = pl.ds(pl.multiple_of(at * block, block), block)
        out[:, columns] = total.astype(out.dtype)
        pltpu.make_async_copy(out.at[:, columns], out_hbm.at[:, columns], store_sem.at[at]).start()

    order = [core * ho + j + owner * (1 - core) * (ho - 1 - 2 * j) for j in range(ho)]

    for source in order:

        @pl.when(source != z)
        def _(source=source):
            for aux in range(2):
                wait_recv(slot(aux, source, y), hz_recv.at[aux, source])
                for other in ys:
                    forward(aux, source, other).start()

    wait_recv(left.at[sib], hs_recv.at[0])

    @pl.when(owner == core)
    def _():
        emit(z, y, left[0], left[1])

    for source in order:

        @pl.when(source != z)
        def _(source=source):
            at = (source % ho) * inner + y
            emit(source, y, h[0, at], h[1, at])

    for source in order:
        for other in ys:
            for aux in range(2):
                wait_recv(slot(aux, source, other), hy_recv.at[aux, source, other])
            at = (source % ho) * inner + other
            emit(source, other, h[0, at], h[1, at])

    for copy in sends:
        copy.wait_send()
    for source in order:

        @pl.when(source != z)
        def _(source=source):
            for aux in range(2):
                for other in ys:
                    forward(aux, source, other).wait_send()

    for at in range(n // 2):
        columns = pl.ds(at * block, block)
        pltpu.make_async_copy(out.at[:, columns], out_hbm.at[:, columns], store_sem.at[at]).wait()


def local(n, integrals, coefficients, screen):
    outer, inner = split_rows(n)
    block, occupied = coefficients.shape
    dma = pltpu.SemaphoreType.DMA
    basis = n * block
    return pl.pallas_call(
        functools.partial(kernel, outer, inner),
        out_shape=jax.ShapeDtypeStruct((block, basis // 2), jnp.bfloat16),
        in_specs=[
            pl.BlockSpec(memory_space=pl.ANY),
            pl.BlockSpec(memory_space=pl.ANY),
            pl.BlockSpec(memory_space=pltpu.SMEM),
        ],
        out_specs=pl.BlockSpec(memory_space=pl.ANY),
        scratch_shapes=[
            pltpu.VMEM((block, basis), jnp.bfloat16),
            pltpu.VMEM((n, block, occupied), jnp.bfloat16),
            pltpu.VMEM((block, occupied), jnp.float32),
            pltpu.VMEM((2, block, occupied), jnp.bfloat16),
            pltpu.VMEM((2, n // 2, block, occupied), jnp.bfloat16),
            pltpu.VMEM((block, basis // 2), jnp.bfloat16),
            dma((2,)),
            dma((n // 2,)),
            dma((outer,)),
            dma((outer,)),
            dma((outer, inner)),
            dma((outer, inner)),
            dma((n,)),
            dma((n,)),
            dma((1,)),
            dma((1,)),
            dma((outer,)),
            dma((2, outer)),
            dma((inner,)),
            dma((2, outer, inner)),
            dma((2, outer, inner)),
        ],
        compiler_params=pltpu.CompilerParams(
            collective_id=0, has_side_effects=True, vmem_limit_bytes=44 * 1024 * 1024
        ),
        cost_estimate=pl.CostEstimate(
            flops=4 * block * basis * occupied, bytes_accessed=4 * block * basis, transcendentals=0
        ),
    )(integrals, coefficients, screen)


def solution(mesh):
    in_specs = (
        P(("parts", "aux"), "rows", None),
        P(("parts", "rows"), None),
        P(("parts", "aux"), "rows", None),
    )
    out_specs = P(("parts", "rows"), "aux")
    body = functools.partial(local, mesh.shape["rows"])
    return jax.shard_map(body, mesh=mesh, in_specs=in_specs, out_specs=out_specs, check_vma=False)
```

time: 111 us -> 40.6 us (0.37)
  the two profiles are of different devices: /device:TPU:1 before, /device:TPU:28 now
where the time goes in v1:
time: 40.6 us; the launch traced here: 40.5 us
  Pallas kernels  36.9 us (91%)
  local copies, waits for them, and re-layouts  3.58 us (9%)
    pallas_call x1, Pallas kernels, local(): pl.pallas_call(functools.partial(kernel, outer, inner), out_shape=jax.Sha...  36.9 us
    unnamed x7, local copies, waits for them, and re-layouts  3.58 us

profile of v1, /device:TPU:28, one launch (start us, length us, event | category | flops | bytes accessed | tf_op | source)
XLA Modules:
  0.0 40.5 jit_solution(9807665356823074293)
XLA Ops:
  0.0 0.0 copy-start
  0.0 1.2 %copy-done = bf16[1,256,2048]{2,1,0:T(8,128)(2,1)S(1)} copy-done((bf16[1,256,2048]{2,1,0:T(8,128)(2,1)S(1)}, bf16[1,256,2048]{2,1,0:T(8,128)(2,1)}, u32[]{:S(2)}) %copy-start) | copy-done | bytes 1048600
  1.2 0.0 copy-start.1
  1.2 0.9 %copy-done.1 = bf16[256,256]{1,0:T(8,128)(2,1)S(1)} copy-done((bf16[256,256]{1,0:T(8,128)(2,1)S(1)}, bf16[256,256]{1,0:T(8,128)(2,1)}, u32[]{:S(2)}) %copy-start.1) | copy-done | bytes 131096
  2.1 0.0 copy-start.2
  2.1 0.7 %copy-done.2 = s32[1,1,8]{2,1,0:T(1,128)S(1)} copy-done((s32[1,1,8]{2,1,0:T(1,128)S(1)}, s32[1,1,8]{2,1,0:T(1,128)}, u32[]{:S(2)}) %copy-start.2) | copy-done | bytes 56
  2.8 36.9 %shard_map.37 = bf16[256,1024]{1,0:T(8,128)(2,1)S(1)} custom-call(bf16[1,256,2048]{2,1,0:T(8,128)(2,1)S(1)} %copy-done, bf16[256,256]{1,0:T(8,128)(2,1)S(1)} %copy-done.1, s32[1,1,8]{2,1,0:T(1,128)S(1)} %copy-done.2), custom_call_target="tpu_custom_call" | custom-call | flops 536870912 | bytes 2097152 | tf_op jit(solution)/shard_map/pallas_call | solution.py:260
  39.7 0.8 %copy.5 = bf16[256,1024]{1,0:T(8,128)(2,1)} copy(bf16[256,1024]{1,0:T(8,128)(2,1)S(1)} %shard_map.37) | data formatting | bytes 1048576
Async XLA Ops:
  0.0 1.2 %copy-start = (bf16[1,256,2048]{2,1,0:T(8,128)(2,1)S(1)}, bf16[1,256,2048]{2,1,0:T(8,128)(2,1)}, u32[]{:S(2)}) copy-start(bf16[1,256,2048]{2,1,0:T(8,128)(2,1)} %a_hbm.1) | copy-start | bytes 3145732
  1.2 0.9 %copy-start.1 = (bf16[256,256]{1,0:T(8,128)(2,1)S(1)}, bf16[256,256]{1,0:T(8,128)(2,1)}, u32[]{:S(2)}) copy-start(bf16[256,256]{1,0:T(8,128)(2,1)} %c_hbm.1) | copy-start | bytes 393220
  2.1 0.7 %copy-start.2 = (s32[1,1,8]{2,1,0:T(1,128)S(1)}, s32[1,1,8]{2,1,0:T(1,128)}, u32[]{:S(2)}) copy-start(s32[1,1,8]{2,1,0:T(1,128)} %screen.1) | copy-start | bytes 100

commit v2 on v1

v2 whole, which is shorter than its diff:
```python
import functools

import jax
import jax.numpy as jnp
from jax import lax
from jax.experimental import pallas as pl
from jax.experimental.pallas import tpu as pltpu
from jax.sharding import PartitionSpec as P

MESH = pl.DeviceIdType.MESH
CHUNKS = 2


def split_rows(n):
    inner = 1
    while inner * inner * 4 <= n:
        inner *= 2
    return n // inner, inner


def table(outer, rank, z):
    code = 0
    for place in range(outer):
        others = sorted((k for k in range(outer) if k != place), key=lambda k: (abs(k - place), k))
        code += others[rank] * outer**place
    power = 1
    bit = 1
    while bit < outer:
        power = power * (1 + (outer**bit - 1) * ((z // bit) % 2))
        bit *= 2
    return (code // power) % outer


def remote(src, dst, send, recv, rows, aux):
    return pltpu.make_async_remote_copy(
        src_ref=src,
        dst_ref=dst,
        send_sem=send,
        recv_sem=recv,
        device_id={"rows": rows, "aux": aux},
        device_id_type=MESH,
    )


def kernel(
    outer,
    inner,
    a_hbm,
    c_hbm,
    screen_hbm,
    out_hbm,
    a,
    screen,
    c_own,
    ct,
    acc,
    own,
    left,
    h,
    out,
    load_sem,
    store_sem,
    a_send,
    a_recv,
    cz_send,
    cz_recv,
    cy_send,
    cy_recv,
    hs_send,
    hs_recv,
    hz_send,
    hz_recv,
    hy_send,
    hf_send,
    hy_recv,
    cf_send,
    ho_send,
):
    n = outer * inner
    block, occupied = c_hbm.shape
    ho = outer // 2
    width = occupied // 2
    ic = width // CHUNKS
    groups = 2 * CHUNKS
    me = lax.axis_index("rows")
    core = lax.axis_index("aux")
    sib = 1 - core
    z = me // inner
    y = me % inner
    owner = z // ho

    mine_i = pl.ds(pl.multiple_of(core * width, width), width)
    load_c = pltpu.make_async_copy(c_hbm.at[:, mine_i], c_own, load_sem.at[1])
    load_a = pltpu.make_async_copy(a_hbm.at[0], a.at[core], load_sem.at[0])
    load_s = pltpu.make_async_copy(screen_hbm, screen, load_sem.at[2])
    load_c.start()
    load_s.start()
    load_a.start()

    zs = [table(outer, rank, z) for rank in range(outer - 1)]
    ys = [(y + k) % inner for k in range(1, inner)]
    hub = outer == 4
    mate = z + 1 - 2 * (z % 2)
    inside = ((z + 1) // 2) % 2
    direct = [2 - z // 2, mate] if hub else zs[::-1]

    barrier = pltpu.get_barrier_semaphore()
    for k in range(2):
        for other in zs:
            pl.semaphore_signal(
                barrier, inc=1, device_id={"rows": other * inner + y, "aux": k}, device_id_type=MESH
            )
        for other in ys:
            pl.semaphore_signal(
                barrier, inc=1, device_id={"rows": z * inner + other, "aux": k}, device_id_type=MESH
            )
    pl.semaphore_signal(barrier, inc=1, device_id={"rows": me, "aux": sib}, device_id_type=MESH)

    load_c.wait()
    turned = c_own[...].T
    for q in range(CHUNKS):
        ct[q, me] = turned[q * ic : (q + 1) * ic]

    pl.semaphore_wait(barrier, 2 * (outer - 1) + 2 * (inner - 1) + 1)

    sends = []

    def start(copy):
        copy.start()
        sends.append(copy)

    def wait_recv(ref, sem):
        remote(ref, ref, a_send.at[0], sem, me, sib).wait_recv()

    def c_along_y(q, source):
        ref = ct.at[q, source * inner + y]
        for other in ys:
            start(
                remote(
                    ref,
                    ref,
                    cy_send.at[q, source, other],
                    cy_recv.at[q, source, y],
                    z * inner + other,
                    core,
                )
            )

    for q in range(CHUNKS):
        for other in direct:
            ref = ct.at[q, me]
            start(remote(ref, ref, cz_send.at[q, other], cz_recv.at[q, z], other * inner + y, core))
        c_along_y(q, z)

    load_s.wait()
    load_a.wait()
    for s in range(n):
        columns = pl.ds(s * block, block)
        flag = screen[0, 0, s].astype(jnp.float32)
        a[core, :, columns] = (a[core, :, columns].astype(jnp.float32) * flag).astype(a.dtype)
    start(remote(a.at[core], a.at[core], a_send.at[0], a_recv.at[0], me, sib))

    def c_onward(q, source):
        ref = ct.at[q, source * inner + y]
        return remote(
            ref, ref, cf_send.at[q, source], cz_recv.at[q, source], mate * inner + y, core
        )

    def c_from_z(q):
        for source in zs:
            wait_recv(ct.at[q, source * inner + y], cz_recv.at[q, source])
            if hub:

                @pl.when((inside == 1) & (source != mate))
                def _(source=source):
                    c_onward(q, source).start()

            c_along_y(q, source)

    nt = (((1,), (1,)), ((), ()))

    def product(q, s, first=False):
        columns = pl.ds(pl.multiple_of(s * block, block), block)
        for aux in range(2):
            term = lax.dot_general(
                ct[q, s], a[aux, :, columns], nt, preferred_element_type=jnp.float32
            )
            if first:
                acc[q, aux] = term
            else:
                acc[q, aux] += term

    def slot(source, yy):
        return (source % ho) * inner + yy

    def finish(q):
        for aux in range(2):
            own[core * CHUNKS + q, aux] = acc[q, aux].astype(own.dtype)
        g = core * CHUNKS + q
        ref = own.at[g]
        dst = h.at[slot(z, y), g]
        for other in direct:
            start(remote(ref, dst, hz_send.at[q, other], hz_recv.at[g, z], other * inner + y, owner))
        for other in ys:
            start(
                remote(ref, dst, hy_send.at[q, other], hy_recv.at[g, z, y], z * inner + other, owner)
            )
        start(remote(ref, ref, hs_send.at[q], hs_recv.at[q], me, sib))

    c_from_z(0)
    wait_recv(a.at[sib], a_recv.at[0])
    product(0, me, True)
    for source in zs:
        product(0, source * inner + y)
    for q in range(CHUNKS):
        if q + 1 < CHUNKS:
            c_from_z(q + 1)
        for source in [z] + zs:
            for other in ys:
                s = source * inner + other
                wait_recv(ct.at[q, s], cy_recv.at[q, source, other])
                product(q, s)
        finish(q)
        if q + 1 < CHUNKS:
            product(q + 1, me, True)
            for source in zs:
                product(q + 1, source * inner + y)

    def forward(g, source, other):
        ref = h.at[slot(source, y), g]
        return remote(
            ref, ref, hf_send.at[g, source, other], hy_recv.at[g, source, y], z * inner + other, core
        )

    def onward(g, source):
        ref = h.at[slot(source, y), g]
        return remote(
            ref, ref, ho_send.at[g, source], hz_recv.at[g, source], mate * inner + y, core
        )

    order = [core * ho + j + owner * (1 - core) * (ho - 1 - 2 * j) for j in range(ho)]

    for q in range(CHUNKS):
        for source in order:

            @pl.when(source != z)
            def _(source=source, q=q):
                for k in range(2):
                    g = k * CHUNKS + q
                    wait_recv(h.at[slot(source, y), g], hz_recv.at[g, source])
                    if hub:

                        @pl.when((inside == 1) & (source != mate))
                        def _(source=source, g=g):
                            onward(g, source).start()

                    for other in ys:
                        forward(g, source, other).start()

    for q in range(CHUNKS):
        wait_recv(own.at[sib * CHUNKS + q], hs_recv.at[q])
    for aux in range(2):
        left[aux] = jnp.concatenate([own[g, aux] for g in range(groups)], axis=0).T

    def emit(at, right):
        total = 0.0
        for aux in range(2):
            whole = jnp.concatenate([right(g, aux) for g in range(groups)], axis=0)
            term = jnp.dot(left[aux], whole, preferred_element_type=jnp.float32)
            total = total + term.astype(out.dtype).astype(jnp.float32)
        columns = pl.ds(pl.multiple_of(at * block, block), block)
        out[:, columns] = total.astype(out.dtype)
        pltpu.make_async_copy(out.at[:, columns], out_hbm.at[:, columns], store_sem.at[at]).start()

    @pl.when(owner == core)
    def _():
        emit(slot(z, y), lambda g, aux: own[g, aux])

    for source in order:

        @pl.when(source != z)
        def _(source=source):
            at = slot(source, y)
            emit(at, lambda g, aux: h[at, g, aux])

    last = [core * ho + j + owner * (1 - core) * (ho - 1 - 2 * j) for j in range(ho)]
    for source in last:
        for other in ys:
            at = slot(source, other)
            for g in range(groups):
                wait_recv(h.at[at, g], hy_recv.at[g, source, other])
            emit(at, lambda g, aux, at=at: h[at, g, aux])

    for copy in sends:
        copy.wait_send()
    if hub:
        for source in zs:

            @pl.when((inside == 1) & (source != mate))
            def _(source=source):
                for q in range(CHUNKS):
                    c_onward(q, source).wait_send()

    for source in order:

        @pl.when(source != z)
        def _(source=source):
            for g in range(groups):
                for other in ys:
                    forward(g, source, other).wait_send()
                if hub:

                    @pl.when((inside == 1) & (source != mate))
                    def _(source=source, g=g):
                        onward(g, source).wait_send()


    for at in range(n // 2):
        columns = pl.ds(at * block, block)
        pltpu.make_async_copy(out.at[:, columns], out_hbm.at[:, columns], store_sem.at[at]).wait()


def local(n, integrals, coefficients, screen):
    outer, inner = split_rows(n)
    block, occupied = coefficients.shape
    dma = pltpu.SemaphoreType.DMA
    basis = n * block
    groups = 2 * CHUNKS
    ic = occupied // groups
    return pl.pallas_call(
        functools.partial(kernel, outer, inner),
        out_shape=jax.ShapeDtypeStruct((block, basis // 2), jnp.bfloat16),
        in_specs=[pl.BlockSpec(memory_space=pltpu.HBM)] * 3,
        out_specs=pl.BlockSpec(memory_space=pl.ANY),
        scratch_shapes=[
            pltpu.VMEM((2, block, basis), jnp.bfloat16),
            pltpu.SMEM(screen.shape, jnp.int32),
            pltpu.VMEM((block, occupied // 2), jnp.bfloat16),
            pltpu.VMEM((CHUNKS, n, ic, block), jnp.bfloat16),
            pltpu.VMEM((CHUNKS, 2, ic, block), jnp.float32),
            pltpu.VMEM((groups, 2, ic, block), jnp.bfloat16),
            pltpu.VMEM((2, block, occupied), jnp.bfloat16),
            pltpu.VMEM((n // 2, groups, 2, ic, block), jnp.bfloat16),
            pltpu.VMEM((block, basis // 2), jnp.bfloat16),
            dma((3,)),
            dma((n // 2,)),
            dma((1,)),
            dma((1,)),
            dma((CHUNKS, outer)),
            dma((CHUNKS, outer)),
            dma((CHUNKS, outer, inner)),
            dma((CHUNKS, outer, inner)),
            dma((CHUNKS,)),
            dma((CHUNKS,)),
            dma((CHUNKS, outer)),
            dma((groups, outer)),
            dma((CHUNKS, inner)),
            dma((groups, outer, inner)),
            dma((groups, outer, inner)),
            dma((CHUNKS, outer)),
            dma((groups, outer)),
        ],
        compiler_params=pltpu.CompilerParams(
            collective_id=0, has_side_effects=True, vmem_limit_bytes=60 * 1024 * 1024
        ),
        cost_estimate=pl.CostEstimate(
            flops=4 * block * basis * occupied, bytes_accessed=4 * block * basis, transcendentals=0
        ),
    )(integrals, coefficients, screen)


def solution(mesh):
    in_specs = (
        P(("parts", "aux"), "rows", None),
        P(("parts", "rows"), None),
        P(("parts", "aux"), "rows", None),
    )
    out_specs = P(("parts", "rows"), "aux")
    body = functools.partial(local, mesh.shape["rows"])
    return jax.shard_map(body, mesh=mesh, in_specs=in_specs, out_specs=out_specs, check_vma=False)
```

time: 40.6 us -> 33.7 us (0.83)
  the two profiles are of different devices: /device:TPU:28 before, /device:TPU:1 now
where the time goes in v2:
time: 33.7 us; the launch traced here: 33.5 us
  Pallas kernels  31.7 us (94%)
  local copies, waits for them, and re-layouts  1.87 us (6%)
    pallas_call x1, Pallas kernels, local(): pl.pallas_call(functools.partial(kernel, outer, inner), out_shape=jax.Sha...  31.7 us
    unnamed x1, local copies, waits for them, and re-layouts  1.87 us

profile of v2, /device:TPU:1, one launch (start us, length us, event | category | flops | bytes accessed | tf_op | source)
XLA Modules:
  0.0 33.5 jit_solution(5118887839279723747)
XLA Ops:
  0.0 31.7 %shard_map.37 = bf16[256,1024]{1,0:T(8,128)(2,1)} custom-call(bf16[1,256,2048]{2,1,0:T(8,128)(2,1)} %a_hbm.1, bf16[256,256]{1,0:T(8,128)(2,1)} %c_hbm.1, s32[1,1,8]{2,1,0:T(1,128)} %screen_hbm.1), custom_call_target="tpu_custom_call" | custom-call | flops 536870912 | bytes 2097152 | tf_op jit(solution)/shard_map/pallas_call | solution.py:330
  31.7 1.9 %copy.5 = bf16[256,1024]{1,0:T(8,128)(2,1)} copy(bf16[256,1024]{1,0:T(8,128)(2,1)} %shard_map.37) | data formatting | bytes 1048576

commit v3 on v2

--- a/solution.py
+++ b/solution.py
@@ -9,6 +9,7 @@
 
 MESH = pl.DeviceIdType.MESH
 CHUNKS = 2
+HUB_C = True
 
 
 def split_rows(n):
@@ -71,10 +72,11 @@
     hz_send,
     hz_recv,
     hy_send,
-    hf_send,
     hy_recv,
     cf_send,
     ho_send,
+    k_send,
+    k_recv,
 ):
     n = outer * inner
     block, occupied = c_hbm.shape
@@ -100,28 +102,41 @@
     zs = [table(outer, rank, z) for rank in range(outer - 1)]
     ys = [(y + k) % inner for k in range(1, inner)]
     hub = outer == 4
+    hub_c = hub and HUB_C
     mate = z + 1 - 2 * (z % 2)
     inside = ((z + 1) // 2) % 2
     direct = [2 - z // 2, mate] if hub else zs[::-1]
 
     barrier = pltpu.get_barrier_semaphore()
+    def greet(rows, aux):
+        pl.semaphore_signal(
+            barrier, inc=1, device_id={"rows": rows, "aux": aux}, device_id_type=MESH
+        )
+
     for k in range(2):
-        for other in zs:
-            pl.semaphore_signal(
-                barrier, inc=1, device_id={"rows": other * inner + y, "aux": k}, device_id_type=MESH
-            )
-        for other in ys:
-            pl.semaphore_signal(
-                barrier, inc=1, device_id={"rows": z * inner + other, "aux": k}, device_id_type=MESH
-            )
-    pl.semaphore_signal(barrier, inc=1, device_id={"rows": me, "aux": sib}, device_id_type=MESH)
+        if hub_c:
+            greet(mate * inner + y, k)
+        else:
+            for other in zs:
+                greet(other * inner + y, k)
+    if hub_c:
+
+        @pl.when(inside == 1)
+        def _():
+            for k in range(2):
+                for j in range(2):
+                    greet((2 * (1 - z // 2) + j) * inner + y, k)
+
+    for other in ys:
+        greet(z * inner + other, core)
+    greet(me, sib)
 
     load_c.wait()
     turned = c_own[...].T
     for q in range(CHUNKS):
         ct[q, me] = turned[q * ic : (q + 1) * ic]
 
-    pl.semaphore_wait(barrier, 2 * (outer - 1) + 2 * (inner - 1) + 1)
+    pl.semaphore_wait(barrier, 2 * (2 if hub_c else outer - 1) + inner)
 
     sends = []
 
@@ -147,7 +162,7 @@
             )
 
     for q in range(CHUNKS):
-        for other in direct:
+        for other in direct if hub_c else zs[::-1]:
             ref = ct.at[q, me]
             start(remote(ref, ref, cz_send.at[q, other], cz_recv.at[q, z], other * inner + y, core))
         c_along_y(q, z)
@@ -169,7 +184,7 @@
     def c_from_z(q):
         for source in zs:
             wait_recv(ct.at[q, source * inner + y], cz_recv.at[q, source])
-            if hub:
+            if hub_c:
 
                 @pl.when((inside == 1) & (source != mate))
                 def _(source=source):
@@ -190,22 +205,27 @@
             else:
                 acc[q, aux] += term
 
-    def slot(source, yy):
-        return (source % ho) * inner + yy
-
     def finish(q):
+        g = core * CHUNKS + q
+        ref = own.at[y, g]
         for aux in range(2):
-            own[core * CHUNKS + q, aux] = acc[q, aux].astype(own.dtype)
-        g = core * CHUNKS + q
-        ref = own.at[g]
-        dst = h.at[slot(z, y), g]
+            own[y, g, aux] = acc[q, aux].astype(own.dtype)
         for other in direct:
-            start(remote(ref, dst, hz_send.at[q, other], hz_recv.at[g, z], other * inner + y, owner))
+            start(
+                remote(
+                    ref,
+                    h.at[z % ho, g],
+                    hz_send.at[q, other],
+                    hz_recv.at[g, z],
+                    other * inner + y,
+                    owner,
+                )
+            )
         for other in ys:
             start(
-                remote(ref, dst, hy_send.at[q, other], hy_recv.at[g, z, y], z * inner + other, owner)
+                remote(ref, ref, hy_send.at[q, other], hy_recv.at[q, y], z * inner + other, core)
             )
-        start(remote(ref, ref, hs_send.at[q], hs_recv.at[q], me, sib))
+        start(remote(ref, ref, hs_send.at[q, y], hs_recv.at[q, y], me, sib))
 
     c_from_z(0)
     wait_recv(a.at[sib], a_recv.at[0])
@@ -226,14 +246,8 @@
             for source in zs:
                 product(q + 1, source * inner + y)
 
-    def forward(g, source, other):
-        ref = h.at[slot(source, y), g]
-        return remote(
-            ref, ref, hf_send.at[g, source, other], hy_recv.at[g, source, y], z * inner + other, core
-        )
-
     def onward(g, source):
-        ref = h.at[slot(source, y), g]
+        ref = h.at[source % ho, g]
         return remote(
             ref, ref, ho_send.at[g, source], hz_recv.at[g, source], mate * inner + y, core
         )
@@ -241,59 +255,82 @@
     order = [core * ho + j + owner * (1 - core) * (ho - 1 - 2 * j) for j in range(ho)]
 
     for q in range(CHUNKS):
-        for source in order:
-
-            @pl.when(source != z)
-            def _(source=source, q=q):
-                for k in range(2):
-                    g = k * CHUNKS + q
-                    wait_recv(h.at[slot(source, y), g], hz_recv.at[g, source])
-                    if hub:
-
-                        @pl.when((inside == 1) & (source != mate))
-                        def _(source=source, g=g):
-                            onward(g, source).start()
-
-                    for other in ys:
-                        forward(g, source, other).start()
-
-    for q in range(CHUNKS):
-        wait_recv(own.at[sib * CHUNKS + q], hs_recv.at[q])
-    for aux in range(2):
-        left[aux] = jnp.concatenate([own[g, aux] for g in range(groups)], axis=0).T
-
-    def emit(at, right):
+        for other in ys:
+            ref = own.at[other, core * CHUNKS + q]
+            wait_recv(ref, hy_recv.at[q, other])
+            start(remote(ref, ref, hs_send.at[q, other], hs_recv.at[q, other], me, sib))
+        if hub:
+            for source in order:
+
+                @pl.when((source != z) & (inside == 1) & (source != mate))
+                def _(source=source, q=q):
+                    for k in range(2):
+                        g = k * CHUNKS + q
+                        wait_recv(h.at[source % ho, g], hz_recv.at[g, source])
+                        onward(g, source).start()
+
+    for yy in [y] + ys:
+        for q in range(CHUNKS):
+            wait_recv(own.at[yy, sib * CHUNKS + q], hs_recv.at[q, yy])
+        for aux in range(2):
+            left[yy, aux] = jnp.concatenate([own[yy, g, aux] for g in range(groups)], axis=0).T
+
+    def columns(source, yy):
+        at = (source % ho) * inner + yy
+        return pl.ds(pl.multiple_of(at * block, block), block)
+
+    def product_of(yy, right):
         total = 0.0
         for aux in range(2):
-            whole = jnp.concatenate([right(g, aux) for g in range(groups)], axis=0)
-            term = jnp.dot(left[aux], whole, preferred_element_type=jnp.float32)
+            whole = jnp.concatenate([right[g, aux] for g in range(groups)], axis=0)
+            term = jnp.dot(left[yy, aux], whole, preferred_element_type=jnp.float32)
             total = total + term.astype(out.dtype).astype(jnp.float32)
-        columns = pl.ds(pl.multiple_of(at * block, block), block)
-        out[:, columns] = total.astype(out.dtype)
-        pltpu.make_async_copy(out.at[:, columns], out_hbm.at[:, columns], store_sem.at[at]).start()
+        return total.astype(out.dtype)
+
+    def theirs(source, other):
+        at = out_hbm.at[:, columns(source, y)]
+        return remote(
+            out.at[source % ho, other],
+            at,
+            k_send.at[source % ho, other],
+            k_recv.at[source % ho, y],
+            z * inner + other,
+            core,
+        )
+
+    def ours(source):
+        return pltpu.make_async_copy(
+            out.at[source % ho, y], out_hbm.at[:, columns(source, y)], store_sem.at[source % ho]
+        )
+
+    def emit(source, right):
+        for other in ys:
+            out[source % ho, other] = product_of(other, right)
+            theirs(source, other).start()
+        out[source % ho, y] = product_of(y, right)
+        ours(source).start()
 
     @pl.when(owner == core)
     def _():
-        emit(slot(z, y), lambda g, aux: own[g, aux])
+        emit(z, own.at[y])
 
     for source in order:
 
         @pl.when(source != z)
         def _(source=source):
-            at = slot(source, y)
-            emit(at, lambda g, aux: h[at, g, aux])
-
-    last = [core * ho + j + owner * (1 - core) * (ho - 1 - 2 * j) for j in range(ho)]
-    for source in last:
-        for other in ys:
-            at = slot(source, other)
-            for g in range(groups):
-                wait_recv(h.at[at, g], hy_recv.at[g, source, other])
-            emit(at, lambda g, aux, at=at: h[at, g, aux])
+            right = h.at[source % ho]
+            skip = (inside == 1) & (source != mate) if hub else False
+
+            @pl.when(jnp.logical_not(skip))
+            def _():
+                for g in range(groups):
+                    wait_recv(right.at[g], hz_recv.at[g, source])
+
+            emit(source, right)
 
     for copy in sends:
         copy.wait_send()
-    if hub:
+    if hub_c:
         for source in zs:
 
             @pl.when((inside == 1) & (source != mate))
@@ -301,23 +338,20 @@
                 for q in range(CHUNKS):
                     c_onward(q, source).wait_send()
 
+    if hub:
+        for source in order:
+
+            @pl.when((source != z) & (inside == 1) & (source != mate))
+            def _(source=source):
+                for g in range(groups):
+                    onward(g, source).wait_send()
+
     for source in order:
-
-        @pl.when(source != z)
-        def _(source=source):
-            for g in range(groups):
-                for other in ys:
-                    forward(g, source, other).wait_send()
-                if hub:
-
-                    @pl.when((inside == 1) & (source != mate))
-                    def _(source=source, g=g):
-                        onward(g, source).wait_send()
-
-
-    for at in range(n // 2):
-        columns = pl.ds(at * block, block)
-        pltpu.make_async_copy(out.at[:, columns], out_hbm.at[:, columns], store_sem.at[at]).wait()
+        ours(source).wait()
+        for other in ys:
+            theirs(source, other).wait_send()
+            at = out_hbm.at[:, columns(source, other)]
+            wait_recv(at, k_recv.at[source % ho, other])
 
 
 def local(n, integrals, coefficients, screen):
@@ -338,27 +372,28 @@
             pltpu.VMEM((block, occupied // 2), jnp.bfloat16),
             pltpu.VMEM((CHUNKS, n, ic, block), jnp.bfloat16),
             pltpu.VMEM((CHUNKS, 2, ic, block), jnp.float32),
-            pltpu.VMEM((groups, 2, ic, block), jnp.bfloat16),
-            pltpu.VMEM((2, block, occupied), jnp.bfloat16),
-            pltpu.VMEM((n // 2, groups, 2, ic, block), jnp.bfloat16),
-            pltpu.VMEM((block, basis // 2), jnp.bfloat16),
+            pltpu.VMEM((inner, groups, 2, ic, block), jnp.bfloat16),
+            pltpu.VMEM((inner, 2, block, occupied), jnp.bfloat16),
+            pltpu.VMEM((outer // 2, groups, 2, ic, block), jnp.bfloat16),
+            pltpu.VMEM((outer // 2, inner, block, block), jnp.bfloat16),
             dma((3,)),
-            dma((n // 2,)),
+            dma((outer // 2,)),
             dma((1,)),
             dma((1,)),
             dma((CHUNKS, outer)),
             dma((CHUNKS, outer)),
             dma((CHUNKS, outer, inner)),
             dma((CHUNKS, outer, inner)),
-            dma((CHUNKS,)),
-            dma((CHUNKS,)),
+            dma((CHUNKS, inner)),
+            dma((CHUNKS, inner)),
             dma((CHUNKS, outer)),
             dma((groups, outer)),
             dma((CHUNKS, inner)),
-            dma((groups, outer, inner)),
-            dma((groups, outer, inner)),
+            dma((CHUNKS, inner)),
             dma((CHUNKS, outer)),
             dma((groups, outer)),
+            dma((outer // 2, inner)),
+            dma((outer // 2, inner)),
         ],
         compiler_params=pltpu.CompilerParams(
             collective_id=0, has_side_effects=True, vmem_limit_bytes=60 * 1024 * 1024

time: 33.7 us -> 32.7 us (0.970)
  Pallas kernels: 31.7 us -> 30.4 us
    pallas_call x1, Pallas kernels: 31.7 us -> 30.4 us  [local(): pl.pallas_call(functools.partial(kernel, outer, inner), out_shape=jax.Sha...]
where the time goes in v3:
time: 32.7 us; the launch traced here: 32.3 us
  Pallas kernels  30.4 us (93%)
  local copies, waits for them, and re-layouts  1.87 us (6%)
    pallas_call x1, Pallas kernels, local(): pl.pallas_call(functools.partial(kernel, outer, inner), out_shape=jax.Sha...  30.4 us
    unnamed x1, local copies, waits for them, and re-layouts  1.87 us

profile of v3, /device:TPU:1, one launch (start us, length us, event | category | flops | bytes accessed | tf_op | source)
XLA Modules:
  0.0 32.3 jit_solution(11028010154885968459)
XLA Ops:
  0.0 30.4 %shard_map.37 = bf16[256,1024]{1,0:T(8,128)(2,1)} custom-call(bf16[1,256,2048]{2,1,0:T(8,128)(2,1)} %a_hbm.1, bf16[256,256]{1,0:T(8,128)(2,1)} %c_hbm.1, s32[1,1,8]{2,1,0:T(1,128)} %screen_hbm.1), custom_call_target="tpu_custom_call" | custom-call | flops 536870912 | bytes 2097152 | tf_op jit(solution)/shard_map/pallas_call | solution.py:364
  30.4 1.9 %copy.5 = bf16[256,1024]{1,0:T(8,128)(2,1)} copy(bf16[256,1024]{1,0:T(8,128)(2,1)} %shard_map.37) | data formatting | bytes 1048576

commit v4 on v3

--- a/solution.py
+++ b/solution.py
@@ -105,6 +105,7 @@
     hub_c = hub and HUB_C
     mate = z + 1 - 2 * (z % 2)
     inside = ((z + 1) // 2) % 2
+    far = 3 * (1 - z // 2)
     direct = [2 - z // 2, mate] if hub else zs[::-1]
 
     barrier = pltpu.get_barrier_semaphore()
@@ -127,6 +128,11 @@
                 for j in range(2):
                     greet((2 * (1 - z // 2) + j) * inner + y, k)
 
+        @pl.when(inside == 0)
+        def _():
+            for k in range(2):
+                greet((2 - z // 2) * inner + y, k)
+
     for other in ys:
         greet(z * inner + other, core)
     greet(me, sib)
@@ -136,7 +142,8 @@
     for q in range(CHUNKS):
         ct[q, me] = turned[q * ic : (q + 1) * ic]
 
-    pl.semaphore_wait(barrier, 2 * (2 if hub_c else outer - 1) + inner)
+    greeters = 2 * (2 + inside) if hub_c else 2 * (outer - 1)
+    pl.semaphore_wait(barrier, greeters + inner)
 
     sends = []
 
@@ -161,11 +168,20 @@
                 )
             )
 
+    def c_far(q):
+        ref = ct.at[q, me]
+        return remote(ref, ref, cz_send.at[q, far], cz_recv.at[q, z], far * inner + y, core)
+
     for q in range(CHUNKS):
         for other in direct if hub_c else zs[::-1]:
             ref = ct.at[q, me]
             start(remote(ref, ref, cz_send.at[q, other], cz_recv.at[q, z], other * inner + y, core))
         c_along_y(q, z)
+        if hub_c:
+
+            @pl.when(inside == 1)
+            def _(q=q):
+                c_far(q).start()
 
     load_s.wait()
     load_a.wait()
@@ -186,7 +202,7 @@
             wait_recv(ct.at[q, source * inner + y], cz_recv.at[q, source])
             if hub_c:
 
-                @pl.when((inside == 1) & (source != mate))
+                @pl.when((inside == 1) & (source == far))
                 def _(source=source):
                     c_onward(q, source).start()
 
@@ -204,6 +220,17 @@
                 acc[q, aux] = term
             else:
                 acc[q, aux] += term
+
+    def h_far(q):
+        g = core * CHUNKS + q
+        return remote(
+            own.at[y, g],
+            h.at[z % ho, g],
+            hz_send.at[q, far],
+            hz_recv.at[g, z],
+            far * inner + y,
+            owner,
+        )
 
     def finish(q):
         g = core * CHUNKS + q
@@ -221,6 +248,12 @@
                     owner,
                 )
             )
+        if hub:
+
+            @pl.when(inside == 1)
+            def _():
+                h_far(q).start()
+
         for other in ys:
             start(
                 remote(ref, ref, hy_send.at[q, other], hy_recv.at[q, y], z * inner + other, core)
@@ -262,7 +295,7 @@
         if hub:
             for source in order:
 
-                @pl.when((source != z) & (inside == 1) & (source != mate))
+                @pl.when((source != z) & (inside == 1) & (source == far))
                 def _(source=source, q=q):
                     for k in range(2):
                         g = k * CHUNKS + q
@@ -319,7 +352,7 @@
         @pl.when(source != z)
         def _(source=source):
             right = h.at[source % ho]
-            skip = (inside == 1) & (source != mate) if hub else False
+            skip = (inside == 1) & (source == far) if hub else False
 
             @pl.when(jnp.logical_not(skip))
             def _():
@@ -330,10 +363,18 @@
 
     for copy in sends:
         copy.wait_send()
+    if hub:
+
+        @pl.when(inside == 1)
+        def _():
+            for q in range(CHUNKS):
+                c_far(q).wait_send()
+                h_far(q).wait_send()
+
     if hub_c:
         for source in zs:
 
-            @pl.when((inside == 1) & (source != mate))
+            @pl.when((inside == 1) & (source == far))
             def _(source=source):
                 for q in range(CHUNKS):
                     c_onward(q, source).wait_send()
@@ -341,7 +382,7 @@
     if hub:
         for source in order:
 
-            @pl.when((source != z) & (inside == 1) & (source != mate))
+            @pl.when((source != z) & (inside == 1) & (source == far))
             def _(source=source):
                 for g in range(groups):
                     onward(g, source).wait_send()

time: 32.7 us -> 31.9 us (0.976)
  Pallas kernels: 30.4 us -> 29.8 us
    pallas_call x1, Pallas kernels: 30.4 us -> 29.8 us  [local(): pl.pallas_call(functools.partial(kernel, outer, inner), out_shape=jax.Sha...]
where the time goes in v4:
time: 31.9 us; the launch traced here: 31.7 us
  Pallas kernels  29.8 us (93%)
  local copies, waits for them, and re-layouts  1.87 us (6%)
    pallas_call x1, Pallas kernels, local(): pl.pallas_call(functools.partial(kernel, outer, inner), out_shape=jax.Sha...  29.8 us
    unnamed x1, local copies, waits for them, and re-layouts  1.87 us

profile of v4, /device:TPU:1, one launch (start us, length us, event | category | flops | bytes accessed | tf_op | source)
XLA Modules:
  0.0 31.7 jit_solution(419959096828994757)
XLA Ops:
  0.0 29.8 %shard_map.37 = bf16[256,1024]{1,0:T(8,128)(2,1)} custom-call(bf16[1,256,2048]{2,1,0:T(8,128)(2,1)} %a_hbm.1, bf16[256,256]{1,0:T(8,128)(2,1)} %c_hbm.1, s32[1,1,8]{2,1,0:T(1,128)} %screen_hbm.1), custom_call_target="tpu_custom_call" | custom-call | flops 536870912 | bytes 2097152 | tf_op jit(solution)/shard_map/pallas_call | solution.py:405
  29.8 1.9 %copy.5 = bf16[256,1024]{1,0:T(8,128)(2,1)} copy(bf16[256,1024]{1,0:T(8,128)(2,1)} %shard_map.37) | data formatting | bytes 1048576
